TPU v7x, 768 devices: a whole 4x8x12 slice. The times are simulated.
768 devices in a mesh: tp: 16 (over y, x_hi), fsdp: 48 (over x_lo, z, core).
Axes of the slice: x: 4 (x_hi: 2, x_lo: 2; x = x_hi * 2 + x_lo), y: 8, z: 12, core: 2. Of those that a mesh axis runs over, the one named last changes fastest.
Arguments:
- tokens: bfloat16 [512, 4608], P(None, 'tp'), may hold values from -6 to 6
- gate_weight: bfloat16 [4608, 36864], P('tp', 'fsdp'), may hold values from -0.09375 to 0.09375
- up_weight: bfloat16 [4608, 36864], P('tp', 'fsdp'), may hold values from -0.09375 to 0.09375
- down_weight: bfloat16 [36864, 4608], P('fsdp', 'tp'), may hold values from -0.03125 to 0.03125
- out_grad: bfloat16 [512, 4608], P(None, 'tp'), may hold values from -6 to 6
Outputs:
- mixed: bfloat16 [512, 4608], P(None, 'tp')
- tokens_grad: bfloat16 [512, 4608], P(None, 'tp')
- gate_grad: float32 [4608, 36864], P('tp', 'fsdp')
- up_grad: float32 [4608, 36864], P('tp', 'fsdp')
- down_grad: float32 [36864, 4608], P('fsdp', 'tp')
All inputs are finite; a program needn't handle non-finite values.
Results may differ from a plain program's by a relative error of at most 0.005.
Values may be sent and summed in bfloat16 or wider, within the bound.
A program may use at most 32 MiB of HBM per device.

v0:
```python
import jax
import jax.numpy as jnp
from jax import lax
from jax.sharding import PartitionSpec as P


def contract_rows(left, right):
    return lax.dot_general(
        left, right, (((0,), (0,)), ((), ())), preferred_element_type=jnp.float32
    )


def contract_cols(left, right):
    return lax.dot_general(
        left, right, (((1,), (1,)), ((), ())), preferred_element_type=jnp.float32
    )


def gating(sums, width):
    gate = sums[:, :width]
    up = sums[:, width : 2 * width]
    hidden_back = sums[:, 2 * width :]
    sig = jax.nn.sigmoid(gate)
    activated = gate * sig
    hidden = (activated * up).astype(jnp.bfloat16)
    up_back = (hidden_back * activated).astype(jnp.bfloat16)
    gate_back = (hidden_back * up * sig * (1.0 + gate * (1.0 - sig))).astype(jnp.bfloat16)
    return jnp.concatenate([hidden, gate_back, up_back], axis=1)


def shards(tokens, gate_weight, up_weight, down_weight, out_grad):
    width = gate_weight.shape[1]
    rows_in = tokens
    rows_back = out_grad
    gate = jnp.dot(rows_in, gate_weight, preferred_element_type=jnp.float32)
    up = jnp.dot(rows_in, up_weight, preferred_element_type=jnp.float32)
    hidden_back = contract_cols(rows_back, down_weight)
    share = lax.psum_scatter(
        jnp.concatenate([gate, up, hidden_back], axis=1), "tp", scatter_dimension=0, tiled=True
    )
    packed = gating(share, width)
    piece = lax.all_gather(packed, "tp", axis=0, tiled=True)
    hidden = piece[:, :width]
    gate_back = piece[:, width : 2 * width]
    up_back = piece[:, 2 * width :]
    rows_in = tokens
    rows_back = out_grad
    mixed_rows = jnp.dot(hidden, down_weight, preferred_element_type=jnp.float32)
    input_rows = contract_cols(gate_back, gate_weight) + contract_cols(up_back, up_weight)
    mixed_part = mixed_rows
    inputs_part = input_rows
    gate_acc = contract_rows(rows_in, gate_back)
    up_acc = contract_rows(rows_in, up_back)
    down_acc = contract_rows(hidden, rows_back)
    result = (mixed_part, inputs_part, gate_acc, up_acc, down_acc)
    mixed_part, inputs_part, gate_grad, up_grad, down_grad = result
    mixed_sum, inputs_sum = lax.psum((mixed_part, inputs_part), "fsdp")
    return (
        mixed_sum.astype(jnp.bfloat16),
        inputs_sum.astype(jnp.bfloat16),
        gate_grad,
        up_grad,
        down_grad,
    )


def solution(mesh):
    placed = (P(None, "tp"), P("tp", "fsdp"), P("tp", "fsdp"), P("fsdp", "tp"), P(None, "tp"))
    return jax.shard_map(
        shards,
        mesh=mesh,
        in_specs=placed,
        out_specs=(P(None, "tp"), P(None, "tp"), P("tp", "fsdp"), P("tp", "fsdp"), P("fsdp", "tp")),
        check_vma=False,
    )
```

profile of v0, /device:TPU:1, one launch (start us, length us, event | category | flops | bytes accessed | tf_op | source)
XLA Modules:
  0.0 530.6 jit_solution(7518875942991160727)
XLA Ops:
  7.2 0.0 copy-start
  7.2 0.0 copy-start.1
  7.2 0.0 copy-start.3
  7.2 0.0 copy-start.4
  7.2 0.0 copy-start.6
  7.2 0.0 reduce-scatter.2.cloned.1.call-start
  7.3 0.9 copy-done
  8.2 1.6 fusion.10
  9.7 0.0 copy-done.1
  9.8 0.0 copy-done.3
  9.8 0.6 fusion.11
  10.4 0.0 copy-done.4
  10.4 0.0 copy-done.6
  10.4 0.6 fusion.12
  11.0 2.4 pad_maximum_fusion
  13.4 0.0 reduce-scatter.2.cloned.1.call-update
  13.5 0.0 all-gather.2.cloned.1.call-start
  13.5 229.2 %reduce-scatter.2.cloned.1.call-done = f32[32,2304]{1,0:T(8,128)} async-done(((f32[512,2304]{1,0:T(8,128)}), f32[32,2304]{1,0:T(8,128)}) %reduce-scatter.2.cloned.1.call-update) | async-done | bytes 294928 | tf_op jit(solution)/shard_map/reduce_scatter | solution.py:38
  242.7 1.0 multiply_convert_fusion.2
  243.7 0.7 pad_maximum_fusion.1
  244.4 0.0 all-gather.2.cloned.1.call-update
  244.4 100.5 %all-gather.2.cloned.1.call-done = bf16[512,2304]{1,0:T(8,128)(2,1)} async-done(((bf16[32,2304]{1,0:T(8,128)(2,1)}), bf16[512,2304]{1,0:T(8,128)(2,1)}) %all-gather.2.cloned.1.call-update) | async-done | bytes 2359312 | tf_op jit(solution)/shard_map/all_gather | solution.py:42
  345.0 0.0 copy-start.2
  345.0 1.7 fusion.3
  346.7 2.4 convolution_add_fusion
  349.1 0.0 copy-done.2
  349.1 0.0 copy-start.5
  349.1 2.3 fusion.7
  351.4 168.5 %all-reduce.2 = (bf16[512,288]{0,1:T(8,128)(2,1)}, bf16[512,288]{0,1:T(8,128)(2,1)}) all-reduce(f32[512,288]{0,1:T(8,128)} %fusion.7, f32[512,288]{0,1:T(8,128)} %convolution_add_fusion), channel_id=1, replica_groups=mesh['tp'=16,'fsdp'=48] {'fsdp'}, use_global_device_ids=true, to_apply=%region_1.0 | all-reduce | flops 294912 | bytes 1769472 | tf_op jit(solution)/shard_map/psum | solution.py:57
  519.9 0.0 copy-done.5
  519.9 1.3 fusion.5
  521.2 1.3 convolution_bitcast_fusion.1
  522.5 1.3 convolution_bitcast_fusion
Async XLA Ops:
  7.2 1.0 copy-start
  7.2 2.6 copy-start.1
  7.2 2.6 copy-start.3
  7.2 3.2 copy-start.4
  7.2 3.2 copy-start.6
  7.2 235.5 %reduce-scatter.2.cloned.1.call-start = ((), (), s32[]{:S(2)}) async-start(), calls=%async_computation.1 | async-start | bytes 5013504 | tf_op jit(solution)/shard_map/reduce_scatter | solution.py:38
  13.5 331.5 %all-gather.2.cloned.1.call-start = ((), (), s32[]{:S(2)}) async-start(), calls=%async_computation.2 | async-start | bytes 2506752 | tf_op jit(solution)/shard_map/all_gather | solution.py:42
  345.0 4.1 copy-start.2
  349.1 170.8 %copy-start.5 = (bf16[512,288]{0,1:T(8,128)(2,1)S(1)}, bf16[512,288]{0,1:T(8,128)(2,1)}, u32[]{:S(2)}) copy-start(bf16[512,288]{0,1:T(8,128)(2,1)} %param.9) | copy-start | bytes 884740
Sparse Core Ops, SparseCore 0:
  13.6 229.0 reduce-scatter.1
  247.6 97.2 all-gather.1
where the time goes:
time: 534 us; the launch traced here: 531 us
  waiting for transfers between devices  330 us (62%)
  blocking collectives  169 us (32%)
  between operations  14.1 us (3%)
  matrix products  13 us (2%)
    reduce_scatter x1, waiting for transfers between devices, shards(): lax.psum_scatter(jnp.concatenate([gate, up, hidden_back], axis=1), 'tp',...  229 us
    psum x1, blocking collectives, shards(): mixed_sum, inputs_sum = lax.psum((mixed_part, inputs_part), 'fsdp')  169 us
    all_gather x1, waiting for transfers between devices, shards(): piece = lax.all_gather(packed, 'tp', axis=0, tiled=True)  101 us
  transfers between devices with their start and end apart: 2, of which 2 were waited for; matrix products, arithmetic and copies ran while one was open for 0% of the time, Pallas kernels for 0%

commit v1 on v0

v1 whole, which is shorter than its diff:
```python
import functools
import heapq

import jax
import jax.numpy as jnp
from jax import lax
from jax.experimental import pallas as pl
from jax.experimental.pallas import tpu as pltpu
from jax.sharding import PartitionSpec as P

MESH = pl.DeviceIdType.MESH
BF, F32 = jnp.bfloat16, jnp.float32
NY, NZ = 8, 12
TOKENS, DM, FF = 512, 288, 768
NC = 2
ROWS = TOKENS // NC
U = ROWS // 16
HALF = FF // 2
W3 = 3 * HALF
NSEM = 80 * NC


def contract(left, right, dims):
    return lax.dot_general(left, right, ((dims[:1], dims[1:]), ((), ())), preferred_element_type=F32)


def gating(sums):
    gate, up, back = sums[:, :HALF], sums[:, HALF : 2 * HALF], sums[:, 2 * HALF :]
    sig = jax.nn.sigmoid(gate)
    activated = gate * sig
    hidden = (activated * up).astype(BF)
    up_back = (back * activated).astype(BF)
    gate_back = (back * up * sig * (1.0 + gate * (1.0 - sig))).astype(BF)
    return hidden, gate_back, up_back


def kernel(
    tok, og, wg, wu, wd,
    mixed, tgrad, gg, ug, dg,
    part, sb1, rb1, sf1, rf1, tx, xr, sx, rx, sb2, rb2, sf2, rf2, gat1, gat2,
    wp, cr, av, xlr, bv, zr, fin, gbuf, ubuf, dbuf,
    ss, rs, ls,
):
    tp, fs = lax.axis_index("tp"), lax.axis_index("fsdp")
    y, xh = tp // 2, tp % 2
    xl, z, co = fs // 24, (fs // 2) % NZ, fs % 2

    def ymod(v):
        return lax.rem(v + 2 * NY, NY)

    def dev(dy=0, dxh=0, dxl=0, dz=0, dco=0):
        ny = ymod(y + dy)
        nxh = 1 - xh if dxh else xh
        nxl = 1 - xl if dxl else xl
        nz = lax.rem(z + dz, NZ)
        nco = 1 - co if dco else co
        return (ny * 2 + nxh, (nxl * NZ + nz) * 2 + nco)

    barrier = pltpu.get_barrier_semaphore()
    peers = [dev(dy=1), dev(dy=-1), dev(dxh=1), dev(dxl=1), dev(dco=1)]
    peers += [dev(dz=d) for d in range(1, NZ)]
    for peer in peers:
        pl.semaphore_signal(barrier, inc=1, device_id=peer, device_id_type=MESH)

    sent = []
    count = [0]

    def send(src, dst, to):
        i = count[0]
        count[0] += 1
        copy = pltpu.make_async_remote_copy(
            src_ref=src, dst_ref=dst, send_sem=ss.at[i], recv_sem=rs.at[i], device_id=to, device_id_type=MESH
        )
        copy.start()
        sent.append(copy)
        return copy

    ZORDER = [6, 5, 7, 4, 8, 3, 9, 2, 10, 1, 11]
    KORDER = [4, 3, -3, 2, -2, 1, -1, 0]

    def partial(st, c):
        rows = pl.ds(c * ROWS, ROWS)
        cols = pl.ds(st * HALF, HALF)
        for at, val in (
            (0, lambda: contract(tok[rows, :], wg[:, cols], (1, 0))),
            (1, lambda: contract(tok[rows, :], wu[:, cols], (1, 0))),
            (2, lambda: contract(og[rows, :], wd[cols, :], (1, 1))),
        ):
            part[st, c, :, :, :, at * HALF : (at + 1) * HALF] = val().reshape(NY, 2, U, HALF)

    def chain(value, long, sb, rb, sf, rf):
        got = {}
        todo = {}
        for sg, d in ((1, 0), (-1, 1)):
            first = 1 if sg == long else 2
            todo[sg] = (d, first)
        for s in range(1, 5):
            for sg in (1, -1):
                d, first = todo[sg]
                if s < first:
                    continue
                owner = ymod(y + sg * (5 - s))
                if s > first:
                    got[sg].wait_recv()
                val = value(owner, sg * (5 - s))
                if s > first:
                    val = val + rb[d, s - 2].astype(F32)
                if s == 4 and sg == long:
                    sf[...] = val
                    got[sg] = send(sf, rf, dev(dy=sg))
                else:
                    sb[d, s - 1] = val.astype(BF)
                    got[sg] = send(sb.at[d, s - 1], rb.at[d, s - 1], dev(dy=sg))
            yield
        for sg in (1, -1):
            got[sg].wait_recv()
        d = 1 if long == 1 else 0
        return value(y, 0) + rf[...] + rb[d, 3].astype(F32)

    def spread(slot, long, arrived):
        got = {}
        for s in range(1, 5):
            for sg in (1, -1):
                if s == 4 and sg != long:
                    continue
                if s > 1:
                    got[sg].wait_recv()
                    arrived(ymod(y - sg * (s - 1)))
                at = slot(ymod(y - sg * (s - 1)))
                got[sg] = send(at, at, dev(dy=sg))
            yield
        got[long].wait_recv()
        arrived(ymod(y - long * 4))
        got[-long].wait_recv()
        arrived(ymod(y + long * 3))

    def keep(at, sums):
        hidden, gate_back, up_back = gating(sums)
        at[:, :HALF] = hidden
        at[:, HALF : 2 * HALF] = gate_back
        at[:, 2 * HALF :] = up_back

    def stream0(c):
        long = 1 if c % 2 == 0 else -1

        def value(owner, _):
            return part[0, c, owner]

        total = yield from chain(value, long, sb1.at[c], rb1.at[c], sf1.at[c], rf1.at[c])
        tx[c] = total
        got = send(tx.at[c, 1 - xh], xr.at[c], dev(dxh=1))
        yield
        got.wait_recv()
        keep(gat1.at[c, y, xh], tx[c, xh] + xr[c])
        got = send(gat1.at[c, y, xh], gat1.at[c, y, xh], dev(dxh=1))
        yield
        got.wait_recv()
        yield from spread(lambda o: gat1.at[c, o], long, lambda o: None)

    def stream1_open(c):
        out = {}
        for k, off in enumerate(KORDER):
            sx[c, k] = part[1, c, ymod(y + off), 1 - xh].astype(BF)
            out[off] = send(sx.at[c, k], rx.at[c, k], dev(dxh=1))
        return out

    def stream1(c, from_x):
        long = -1 if c % 2 == 0 else 1
        ready = set()

        def value(owner, off):
            off = 4 if off == -4 else off
            if off not in ready:
                from_x[off].wait_recv()
                ready.add(off)
            k = KORDER.index(off)
            return part[1, c, owner, xh] + rx[c, k].astype(F32)

        yield
        total = yield from chain(value, long, sb2.at[c], rb2.at[c], sf2.at[c], rf2.at[c])
        keep(gat2.at[c, y, xh], total)
        back = []

        def arrived(o):
            back.append(send(gat2.at[c, o, xh], gat2.at[c, o, xh], dev(dxh=1)))

        arrived(y)
        yield from spread(lambda o: gat2.at[c, o, xh], long, arrived)
        yield
        for copy in back:
            copy.wait_recv()

    def reduce(c):
        one = gat1[c].reshape(ROWS, W3)
        two = gat2[c].reshape(ROWS, W3)

        def put(m, val):
            for h in range(2):
                rows = val[h * (ROWS // 2) : (h + 1) * (ROWS // 2)]
                wp[c, m, h, 0] = rows[:, :128]
                wp[c, m, h, 1] = rows[:, 128:256]
                wp[c, m, h, 2, :, :32] = rows[:, 256:]
                wp[c, m, h, 2, :, 32:] = jnp.zeros((ROWS // 2, 96), F32)

        put(0, contract(one[:, :HALF], wd[:HALF, :], (1, 0)) + contract(two[:, :HALF], wd[HALF:, :], (1, 0)))
        put(
            1,
            contract(one[:, HALF : 2 * HALF], wg[:, :HALF], (1, 1))
            + contract(two[:, HALF : 2 * HALF], wg[:, HALF:], (1, 1))
            + contract(one[:, 2 * HALF :], wu[:, :HALF], (1, 1))
            + contract(two[:, 2 * HALF :], wu[:, HALF:], (1, 1)),
        )
        got = send(wp.at[c, 1 - co], cr.at[c], dev(dco=1))
        yield
        got.wait_recv()
        av[c] = wp[c, co, 1 - xl] + cr[c, 1 - xl]
        got = send(av.at[c], xlr.at[c], dev(dxl=1))
        yield
        got.wait_recv()
        bv[c] = (wp[c, co, xl] + cr[c, xl] + xlr[c]).reshape(NZ, ROWS // 8, 128)
        gots = [send(bv.at[c, lax.rem(z + d, NZ)], zr.at[c, d - 1], dev(dz=d)) for d in ZORDER]
        yield
        for copy in gots:
            copy.wait_recv()
        total = bv[c, z]
        for d in range(NZ - 1):
            total = total + zr[c, d]
        fin[c, co, xl, z] = total.astype(BF)
        mine = fin.at[c, co, xl, z]
        gots = [send(mine, mine, dev(dz=d)) for d in ZORDER]
        yield
        for copy in gots:
            copy.wait_recv()
        mine = fin.at[c, co, xl]
        across = send(mine, mine, dev(dxl=1))
        near = send(mine, mine, dev(dco=1))
        yield
        across.wait_recv()
        mine = fin.at[c, co, 1 - xl]
        far = send(mine, mine, dev(dco=1))
        yield
        near.wait_recv()
        far.wait_recv()
        for m, out in ((0, mixed), (1, tgrad)):
            for h in range(2):
                rows = pl.ds(c * ROWS + h * (ROWS // 2), ROWS // 2)
                block = fin[c, m, h].reshape(3, ROWS // 2, 128)
                out[rows, 0:128] = block[0]
                out[rows, 128:256] = block[1]
                out[rows, 256:288] = block[2, :, :32]

    local = []

    def weight_grads():
        for st, g in ((0, gat1), (1, gat2)):
            cols = pl.ds(st * HALF, HALF)
            whole = g[...].reshape(TOKENS, W3)
            gbuf[:, cols] = contract(tok[...], whole[:, HALF : 2 * HALF], (0, 0))
            ubuf[:, cols] = contract(tok[...], whole[:, 2 * HALF :], (0, 0))
            dbuf[cols, :] = contract(whole[:, :HALF], og[...], (0, 0))
        for i, (a, b) in enumerate(((gbuf, gg), (ubuf, ug), (dbuf, dg))):
            copy = pltpu.make_async_copy(a, b, ls.at[i])
            copy.start()
            local.append(copy)

    partial(1, 0)
    pl.semaphore_wait(barrier, len(peers))
    opened = [stream1_open(0)]
    partial(0, 0)
    first = stream0(0)
    next(first)
    tasks = {("a", 0): first}
    for c in range(1, NC):
        partial(1, c)
        opened.append(stream1_open(c))
        partial(0, c)
        tasks["a", c] = stream0(c)
        next(tasks["a", c])
    for c in range(NC):
        tasks["b", c] = stream1(c, opened[c])
        next(tasks["b", c])

    def step(task):
        try:
            next(task)
            return True
        except StopIteration:
            return False

    def chunk(c):
        live = [tasks["a", c], tasks["b", c]]
        while live:
            live = [t for t in live if step(t)]
            yield
        yield from reduce(c)

    def last():
        while True:
            if state["gathered"] == NC:
                weight_grads()
                return
            yield

    live = [chunk(c) for c in range(NC)]
    rounds = 0
    done_grads = False
    while live:
        live = [t for t in live if step(t)]
        rounds += 1
        if rounds == GRADS_AT:
            weight_grads()
            done_grads = True
    if not done_grads:
        weight_grads()
    for copy in sent:
        copy.wait_send()
    for copy in local:
        copy.wait()


GRADS_AT = 99


def shards(tokens, gate_weight, up_weight, down_weight, out_grad):
    vm = pl.BlockSpec(memory_space=pltpu.VMEM)
    hbm = pl.BlockSpec(memory_space=pl.ANY)
    V = pltpu.VMEM
    q = ROWS // 2
    return pl.pallas_call(
        kernel,
        out_shape=(
            jax.ShapeDtypeStruct((TOKENS, DM), BF),
            jax.ShapeDtypeStruct((TOKENS, DM), BF),
            jax.ShapeDtypeStruct((DM, FF), F32),
            jax.ShapeDtypeStruct((DM, FF), F32),
            jax.ShapeDtypeStruct((FF, DM), F32),
        ),
        in_specs=[vm] * 5,
        out_specs=(vm, vm, hbm, hbm, hbm),
        scratch_shapes=[
            V((2, NC, NY, 2, U, W3), F32),
            V((NC, 2, 4, 2, U, W3), BF),
            V((NC, 2, 4, 2, U, W3), BF),
            V((NC, 2, U, W3), F32),
            V((NC, 2, U, W3), F32),
            V((NC, 2, U, W3), F32),
            V((NC, U, W3), F32),
            V((NC, NY, U, W3), BF),
            V((NC, NY, U, W3), BF),
            V((NC, 2, 4, U, W3), BF),
            V((NC, 2, 4, U, W3), BF),
            V((NC, U, W3), F32),
            V((NC, U, W3), F32),
            V((NC, NY, 2, U, W3), BF),
            V((NC, NY, 2, U, W3), BF),
            V((NC, 2, 2, 3, q, 128), F32),
            V((NC, 2, 3, q, 128), F32),
            V((NC, 3, q, 128), F32),
            V((NC, 3, q, 128), F32),
            V((NC, NZ, q // 4, 128), F32),
            V((NC, NZ - 1, q // 4, 128), F32),
            V((NC, 2, 2, NZ, q // 4, 128), BF),
            V((DM, FF), F32),
            V((DM, FF), F32),
            V((FF, DM), F32),
            pltpu.SemaphoreType.DMA((NSEM,)),
            pltpu.SemaphoreType.DMA((NSEM,)),
            pltpu.SemaphoreType.DMA((3,)),
        ],
        compiler_params=pltpu.CompilerParams(
            collective_id=0, has_side_effects=True, vmem_limit_bytes=56 << 20
        ),
        name="swiglu",
    )(tokens, out_grad, gate_weight, up_weight, down_weight)


def solution(mesh):
    placed = (P(None, "tp"), P("tp", "fsdp"), P("tp", "fsdp"), P("fsdp", "tp"), P(None, "tp"))
    return jax.shard_map(
        shards,
        mesh=mesh,
        in_specs=placed,
        out_specs=(P(None, "tp"), P(None, "tp"), P("tp", "fsdp"), P("tp", "fsdp"), P("fsdp", "tp")),
        check_vma=False,
    )
```

time: 534 us -> 125 us (0.23)
  waiting for transfers between devices: 330 us -> 0 us
  blocking collectives: 169 us -> 0 us
  Pallas kernels: 0 us -> 112 us
  between operations: 14.1 us -> 0.66 us
  matrix products: 13 us -> 0 us
  local copies, waits for them, and re-layouts: 0.95 us -> 12.3 us
    reduce_scatter x1 -> x0, waiting for transfers between devices: 229 us -> none  [shards(): lax.psum_scatter(jnp.concatenate([gate, up, hidden_back], axis=1), 'tp',...]
    psum x1 -> x0, blocking collectives: 169 us -> none  [shards(): mixed_sum, inputs_sum = lax.psum((mixed_part, inputs_part), 'fsdp')]
    pallas_call x0 -> x1, Pallas kernels: none -> 112 us  [shards(): pl.pallas_call(kernel, out_shape=(jax.ShapeDtypeStruct((TOKENS, DM), BF),...]
    all_gather x1 -> x0, waiting for transfers between devices: 101 us -> none  [shards(): piece = lax.all_gather(packed, 'tp', axis=0, tiled=True)]
    dot_general x9 -> x0, matrix products: 13 us -> none  [the longest x3 4.67 us: contract_cols(): lax.dot_general(left, right, (((1,), (1,)), ((), ())), preferred_element_...]
    unnamed x14 -> x13, local copies, waits for them, and re-layouts: 0.95 us -> 7.28 us
  transfers between devices with their start and end apart: 2 -> 0, of which waited for: 2 -> 0; matrix products, arithmetic and copies ran while one was open for 0% -> 0% of each run, Pallas kernels for 0% -> 0%
where the time goes in v1:
time: 125 us
  Pallas kernels  112 us (90%)
  local copies, waits for them, and re-layouts  12.3 us (10%)
    pallas_call x1, Pallas kernels, shards(): pl.pallas_call(kernel, out_shape=(jax.ShapeDtypeStruct((TOKENS, DM), BF),...  112 us
    unnamed x13, local copies, waits for them, and re-layouts  7.28 us
    pallas_call x3, local copies, waits for them, and re-layouts, shards(): pl.pallas_call(kernel, out_shape=(jax.ShapeDtypeStruct((TOKENS, DM), BF),...  5.06 us

profile of v1, /device:TPU:1, one launch (start us, length us, event | category | flops | bytes accessed | tf_op | source)
XLA Modules:
  0.0 125.0 jit_solution(14706356289106648112)
XLA Ops:
  0.6 0.0 copy-start.3
  0.6 1.9 %copy.10.tok = bf16[512,288]{1,0:T(8,128)(2,1)} copy(bf16[512,288]{0,1:T(8,128)(2,1)} %param.5) | data formatting | bytes 589824 | tf_op args[0]
  2.6 1.9 %copy.11.og = bf16[512,288]{1,0:T(8,128)(2,1)} copy(bf16[512,288]{0,1:T(8,128)(2,1)} %param.9) | data formatting | bytes 589824 | tf_op args[4]
  4.5 0.0 copy-done.3
  4.5 1.1 copy.12.wd
  5.5 112.0 %swiglu.1 = (bf16[512,288]{1,0:T(8,128)(2,1)}, bf16[512,288]{1,0:T(8,128)(2,1)}, f32[288,768]{1,0:T(8,128)}, f32[288,768]{1,0:T(8,128)}, f32[768,288]{1,0:T(8,128)}) custom-call(bf16[512,288]{1,0:T(8,128)(2,1)} %copy.10.tok, bf16[512,288]{1,0:T(8,128)(2,1)} %copy.11.og, bf16[288,768]{1,0:T(8,128)(2,1)} %wg.1, bf16[288,768]{1,0:T(8,128)(2,1)} %wu.1, ...), custom_call_target="tpu_custom_call" | custom-call | tf_op jit(solution)/shard_map/swiglu/pallas_call | solution.py:329
  117.5 0.0 copy-start
  117.5 2.0 %copy.13 = bf16[512,288]{0,1:T(8,128)(2,1)} copy(bf16[512,288]{1,0:T(8,128)(2,1)} %get-tuple-element.5) | data formatting | bytes 589824 | tf_op jit(solution)/shard_map/swiglu/pallas_call | solution.py:329
  119.5 1.9 %copy.14 = bf16[512,288]{0,1:T(8,128)(2,1)} copy(bf16[512,288]{1,0:T(8,128)(2,1)} %get-tuple-element.6) | data formatting | bytes 589824 | tf_op jit(solution)/shard_map/swiglu/pallas_call | solution.py:329
  121.3 0.0 copy-done
  121.3 0.0 copy-start.2
  121.4 1.3 %copy.15 = f32[768,288]{0,1:T(8,128)} copy(f32[768,288]{1,0:T(8,128)S(1)} %copy-done) | data formatting | bytes 1769472 | tf_op jit(solution)/shard_map/swiglu/pallas_call | solution.py:329
  122.6 0.0 copy-done.2
  122.6 0.0 copy-start.1
  122.6 0.9 copy.18
  123.5 0.6 copy-done.1
  124.1 0.9 copy.19
Async XLA Ops:
  0.6 3.8 %copy-start.3 = (bf16[768,288]{0,1:T(8,128)(2,1)S(1)}, bf16[768,288]{0,1:T(8,128)(2,1)}, u32[]{:S(2)}) copy-start(bf16[768,288]{0,1:T(8,128)(2,1)} %param.8) | copy-start | bytes 1327108
  117.5 3.8 %copy-start = (f32[768,288]{1,0:T(8,128)S(1)}, f32[768,288]{1,0:T(8,128)}, u32[]{:S(2)}) copy-start(f32[768,288]{1,0:T(8,128)} %get-tuple-element.9) | copy-start | bytes 2654212
  121.3 1.3 %copy-start.2 = (f32[288,768]{1,0:T(8,128)S(1)}, f32[288,768]{1,0:T(8,128)}, u32[]{:S(2)}) copy-start(f32[288,768]{1,0:T(8,128)} %get-tuple-element.17) | copy-start | bytes 2654212
  122.6 1.5 %copy-start.1 = (f32[288,768]{1,0:T(8,128)S(1)}, f32[288,768]{1,0:T(8,128)}, u32[]{:S(2)}) copy-start(f32[288,768]{1,0:T(8,128)} %get-tuple-element.18) | copy-start | bytes 2654212

commit v2 on v1

v2 whole, which is shorter than its diff:
```python
import heapq

import jax
import jax.numpy as jnp
from jax import lax
from jax.experimental import pallas as pl
from jax.experimental.pallas import tpu as pltpu
from jax.sharding import PartitionSpec as P

MESH = pl.DeviceIdType.MESH
BF, F32 = jnp.bfloat16, jnp.float32
NY, NZ = 8, 12
TOKENS, DM, FF = 512, 288, 768
NC = 2
ROWS = TOKENS // NC
U = ROWS // 16
HALF = FF // 2
W3 = 3 * HALF
Q = ROWS // 2
NSEM = 45 * NC
LAG, T_Y, T_X, T_CORE, T_XL, T_Z = 1.5, 4.0, 4.5, 2.5, 3.6, 5.0
T_OPEN = (3.5, 5.0)


def contract(left, right, dims):
    return lax.dot_general(left, right, ((dims[:1], dims[1:]), ((), ())), preferred_element_type=F32)


def gating(sums):
    gate, up, back = sums[:, :HALF], sums[:, HALF : 2 * HALF], sums[:, 2 * HALF :]
    sig = jax.nn.sigmoid(gate)
    activated = gate * sig
    hidden = (activated * up).astype(BF)
    up_back = (back * activated).astype(BF)
    gate_back = (back * up * sig * (1.0 + gate * (1.0 - sig))).astype(BF)
    return hidden, gate_back, up_back


def kernel(
    tok_h, og_h, wg_h, wu_h, wd_h,
    mixed, tgrad, gg, ug, dg,
    part, sb1, rb1, sf1, rf1, tx, xr, sx, rx, sb2, rb2, sf2, rf2, gat1, gat2,
    wp, cr, av, xlr, bv, bs, zr, fin, gbuf, ubuf, dbuf, tok, og, tok_t, og_t, wg, wu, wd,
    ss, rs, ls, ins,
):
    tp, fs = lax.axis_index("tp"), lax.axis_index("fsdp")
    y, xh = tp // 2, tp % 2
    xl, z, co = fs // 24, (fs // 2) % NZ, fs % 2

    def ymod(v):
        return lax.rem(v + 2 * NY, NY)

    def dev(dy=0, dxh=0, dxl=0, dz=0, dco=0):
        ny = ymod(y + dy)
        nxh = 1 - xh if dxh else xh
        nxl = 1 - xl if dxl else xl
        nz = lax.rem(z + dz, NZ)
        nco = 1 - co if dco else co
        return (ny * 2 + nxh, (nxl * NZ + nz) * 2 + nco)

    barrier = pltpu.get_barrier_semaphore()
    peers = [dev(dy=1), dev(dy=-1), dev(dxh=1), dev(dxl=1), dev(dco=1)]
    peers += [dev(dz=d) for d in range(1, NZ)]
    for peer in peers:
        pl.semaphore_signal(barrier, inc=1, device_id=peer, device_id_type=MESH)

    loads = {}
    for i, (name, a, b) in enumerate(
        (("tok", tok_h, tok_t), ("wg", wg_h, wg), ("wu", wu_h, wu), ("og", og_h, og_t), ("wd", wd_h, wd))
    ):
        loads[name] = pltpu.make_async_copy(a, b, ins.at[i])
        loads[name].start()

    sent = []
    count = [0]

    def send(src, dst, to, at=None):
        i = count[0] if at is None else at
        count[0] += at is None
        copy = pltpu.make_async_remote_copy(
            src_ref=src, dst_ref=dst, send_sem=ss.at[i], recv_sem=rs.at[i], device_id=to, device_id_type=MESH
        )
        copy.start()
        if at is None:
            sent.append(copy)
        return copy

    def group(whole):
        i = count[0]
        count[0] += 1
        copy = pltpu.make_async_remote_copy(
            src_ref=whole, dst_ref=whole, send_sem=ss.at[i], recv_sem=rs.at[i], device_id=dev(dy=1), device_id_type=MESH
        )
        sent.append(copy)
        return i, copy

    ZORDER = [6, 5, 7, 4, 8, 3, 9, 2, 10, 1, 11]
    KORDER = [4, 3, -3, 2, -2, 1, -1, 0]

    def partial(st, c):
        rows = pl.ds(c * ROWS, ROWS)
        cols = pl.ds(st * HALF, HALF)
        for at, val in (
            (0, lambda: contract(tok[rows, :], wg[:, cols], (1, 0))),
            (1, lambda: contract(tok[rows, :], wu[:, cols], (1, 0))),
            (2, lambda: contract(og[rows, :], wd[:, cols], (1, 0))),
        ):
            part[st, c, :, :, :, at * HALF : (at + 1) * HALF] = val().reshape(NY, 2, U, HALF)

    def chain(value, long, sb, rb, sf, rf):
        got = {}
        todo = {}
        for sg, d in ((1, 0), (-1, 1)):
            first = 1 if sg == long else 2
            todo[sg] = (d, first)
        for s in range(1, 5):
            for sg in (1, -1):
                d, first = todo[sg]
                if s < first:
                    continue
                owner = ymod(y + sg * (5 - s))
                if s > first:
                    got[sg].wait_recv()
                val = value(owner, sg * (5 - s))
                if s > first:
                    val = val + rb[d, s - 2].astype(F32)
                if s == 4:
                    sf[d] = val
                    got[sg] = send(sf.at[d], rf.at[d], dev(dy=sg))
                else:
                    sb[d, s - 1] = val.astype(BF)
                    got[sg] = send(sb.at[d, s - 1], rb.at[d, s - 1], dev(dy=sg))
            yield T_Y
        for sg in (1, -1):
            got[sg].wait_recv()
        return value(y, 0) + rf[0] + rf[1]

    def spread(slot, long, arrived):
        got = {}
        for s in range(1, 5):
            for sg in (1, -1):
                if s == 4 and sg != long:
                    continue
                if s > 1:
                    got[sg].wait_recv()
                    arrived(ymod(y - sg * (s - 1)))
                at = slot(ymod(y - sg * (s - 1)))
                got[sg] = send(at, at, dev(dy=sg))
            yield T_Y
        got[long].wait_recv()
        arrived(ymod(y - long * 4))
        got[-long].wait_recv()
        arrived(ymod(y + long * 3))

    def keep(at, sums):
        hidden, gate_back, up_back = gating(sums)
        at[:, :HALF] = hidden
        at[:, HALF : 2 * HALF] = gate_back
        at[:, 2 * HALF :] = up_back

    def stream0(c):
        long = 1 if c % 2 == 0 else -1

        def value(owner, _):
            return part[0, c, owner]

        total = yield from chain(value, long, sb1.at[c], rb1.at[c], sf1.at[c], rf1.at[c])
        tx[c] = total
        got = send(tx.at[c], xr.at[c], dev(dxh=1))
        yield T_X
        got.wait_recv()
        for h in range(2):
            keep(gat1.at[c, y, h], tx[c, h] + xr[c, h])
        yield from spread(lambda o: gat1.at[c, o], long, lambda o: None)

    def stream1_open(c, out, ks):
        for k in ks:
            off = KORDER[k]
            sx[c, k] = part[1, c, ymod(y + off), 1 - xh].astype(BF)
            out[off] = send(sx.at[c, k], rx.at[c, k], dev(dxh=1))

    def stream1(c, from_x):
        long = -1 if c % 2 == 0 else 1
        ready = set()

        def value(owner, off):
            off = 4 if off == -4 else off
            if off not in ready:
                from_x[off].wait_recv()
                ready.add(off)
            k = KORDER.index(off)
            return part[1, c, owner, xh] + rx[c, k].astype(F32)

        yield T_OPEN[c]
        total = yield from chain(value, long, sb2.at[c], rb2.at[c], sf2.at[c], rf2.at[c])
        keep(gat2.at[c, y, xh], total)
        i, back = group(gat2.at[c, :, 1 - xh])

        def arrived(o):
            send(gat2.at[c, o, xh], gat2.at[c, o, xh], dev(dxh=1), i)

        arrived(y)
        yield from spread(lambda o: gat2.at[c, o, xh], long, arrived)
        yield T_X
        back.wait_recv()

    grads = []

    def weight_grad(i):
        left, cols, out, to = (
            (tok_t, 1, gbuf, gg),
            (tok_t, 2, ubuf, ug),
            (og_t, 0, dbuf, dg),
        )[i]
        for st, g in ((0, gat1), (1, gat2)):
            right = g[:, :, :, :, cols * HALF : (cols + 1) * HALF].reshape(TOKENS, HALF)
            out[:, st * HALF : (st + 1) * HALF] = contract(left[...], right, (1, 0))
        copy = pltpu.make_async_copy(out, to, ls.at[i])
        copy.start()
        local.append(copy)

    local = []

    def weight_grads():
        for i in range(3):
            weight_grad(i)
            yield 3.0

    def flush(c):
        if c == NC - 1:
            while len(sent) > 20:
                sent.pop(0).wait_send()

    def reduce(c):
        def side(weights, at):
            total = None
            for st, g in ((0, gat1), (1, gat2)):
                left = weights[:, st * HALF : (st + 1) * HALF]
                right = g[c, :, :, :, at * HALF : (at + 1) * HALF].reshape(ROWS, HALF)
                one = contract(left, right, (1, 1))
                total = one if total is None else total + one
            return total

        def put(m, val):
            for h in range(2):
                wp[c, m, h] = val[:, h * Q : (h + 1) * Q]

        put(0, side(wd, 0))
        put(1, side(wg, 1) + side(wu, 2))
        got = send(wp.at[c, 1 - co], cr.at[c], dev(dco=1))
        yield T_CORE
        got.wait_recv()
        av[c] = (wp[c, co, 1 - xl] + cr[c, 1 - xl]).astype(BF)
        got = send(av.at[c], xlr.at[c], dev(dxl=1))
        own = wp[c, co, xl] + cr[c, xl]
        wp[c, co, xl] = own
        yield T_XL
        got.wait_recv()
        own = (wp[c, co, xl] + xlr[c].astype(F32)).reshape(NZ, DM // NZ, Q)
        bv[c] = own
        bs[c, :, : DM // NZ] = own.astype(BF)
        i, got = group(zr.at[c])
        for d in ZORDER:
            send(bs.at[c, lax.rem(z + d, NZ)], zr.at[c, d - 1], dev(dz=d), i)
        flush(c)
        yield T_Z
        total = bv[c, z]
        got.wait_recv()
        for d in range(1, NZ):
            total = total + zr[c, d - 1, : DM // NZ].astype(F32)
        fin[c, co, xl, z, : DM // NZ] = total.astype(BF)
        mine = fin.at[c, co, xl, z]
        i, got = group(fin.at[c, co, xl, : NZ - 1])
        for d in ZORDER:
            send(mine, mine, dev(dz=d), i)
        flush(c)
        yield T_Z
        got.wait_recv()
        mine = fin.at[c, co, xl]
        across = send(mine, mine, dev(dxl=1))
        near = send(mine, mine, dev(dco=1))
        flush(c)
        yield T_XL
        across.wait_recv()
        mine = fin.at[c, co, 1 - xl]
        far = send(mine, mine, dev(dco=1))
        yield T_CORE
        near.wait_recv()
        far.wait_recv()
        for m, out in ((0, mixed), (1, tgrad)):
            for h in range(2):
                block = fin[c, m, h, :, : DM // NZ].reshape(DM, Q)
                out[:, c * ROWS + h * Q : c * ROWS + (h + 1) * Q] = block

    queue = []
    left = {c: 2 for c in range(NC)}

    def push(t, task, c, part):
        heapq.heappush(queue, (t, len(order), task, c, part))
        order.append(part)

    order = []
    opened = [{} for _ in range(NC)]

    def opening(c, at):
        if c == 0:
            loads["tok"].wait()
            tok[...] = tok_t[...].T
            loads["wg"].wait()
            loads["wu"].wait()
            loads["og"].wait()
            loads["wd"].wait()
            og[...] = og_t[...].T
        partial(0, c)
        if c == 0:
            pl.semaphore_wait(barrier, len(peers))
        push(at, stream0(c), c, True)
        yield 0.5
        partial(1, c)
        stream1_open(c, opened[c], range(5))
        push(at + 0.5, stream1(c, opened[c]), c, True)
        if c == NC - 1:
            for other in range(NC):
                stream1_open(other, opened[other], range(5, NY))
            fin[...] = jnp.zeros_like(fin)
            bs[...] = jnp.zeros_like(bs)

    for c in range(NC):
        push(c * LAG, opening(c, c * LAG), c, False)
    while queue:
        t, _, task, c, part_of = heapq.heappop(queue)
        try:
            push(t + next(task), task, c, part_of)
        except StopIteration:
            if part_of:
                left[c] -= 1
                if left[c] == 0:
                    push(t, reduce(c), c, False)
                    if not any(left.values()):
                        push(t + 0.1, weight_grads(), NC, False)
    for copy in sent:
        copy.wait_send()
    for copy in local:
        copy.wait()


def hand_over(*refs):
    held, sems = refs[10:15], refs[15]
    into = [pltpu.make_async_copy(refs[i], held[i], sems.at[0, i]) for i in range(5)]
    out = [pltpu.make_async_copy(held[i], refs[5 + i], sems.at[1, i]) for i in range(5)]
    for copy in into:
        copy.start()
    for first, second in zip(into, out):
        first.wait()
        second.start()
    for copy in out:
        copy.wait()


def shards(tokens, gate_weight, up_weight, down_weight, out_grad):
    vm = pl.BlockSpec(memory_space=pltpu.VMEM)
    hbm = pl.BlockSpec(memory_space=pl.ANY)
    V = pltpu.VMEM
    outs = pl.pallas_call(
        kernel,
        out_shape=(
            jax.ShapeDtypeStruct((DM, TOKENS), BF),
            jax.ShapeDtypeStruct((DM, TOKENS), BF),
            jax.ShapeDtypeStruct((DM, FF), F32),
            jax.ShapeDtypeStruct((DM, FF), F32),
            jax.ShapeDtypeStruct((DM, FF), F32),
        ),
        in_specs=[hbm] * 5,
        out_specs=(vm, vm, hbm, hbm, hbm),
        scratch_shapes=[
            V((2, NC, NY, 2, U, W3), F32),
            V((NC, 2, 3, 2, U, W3), BF),
            V((NC, 2, 3, 2, U, W3), BF),
            V((NC, 2, 2, U, W3), F32),
            V((NC, 2, 2, U, W3), F32),
            V((NC, 2, U, W3), F32),
            V((NC, 2, U, W3), F32),
            V((NC, NY, U, W3), BF),
            V((NC, NY, U, W3), BF),
            V((NC, 2, 3, U, W3), BF),
            V((NC, 2, 3, U, W3), BF),
            V((NC, 2, U, W3), F32),
            V((NC, 2, U, W3), F32),
            V((NC, NY, 2, U, W3), BF),
            V((NC, NY, 2, U, W3), BF),
            V((NC, 2, 2, DM, Q), F32),
            V((NC, 2, DM, Q), F32),
            V((NC, DM, Q), BF),
            V((NC, DM, Q), BF),
            V((NC, NZ, DM // NZ, Q), F32),
            V((NC, NZ, 32, Q), BF),
            V((NC, NZ - 1, 32, Q), BF),
            V((NC, 2, 2, NZ, 32, Q), BF),
            V((DM, FF), F32),
            V((DM, FF), F32),
            V((DM, FF), F32),
            V((TOKENS, DM), BF),
            V((TOKENS, DM), BF),
            V((DM, TOKENS), BF),
            V((DM, TOKENS), BF),
            V((DM, FF), BF),
            V((DM, FF), BF),
            V((DM, FF), BF),
            pltpu.SemaphoreType.DMA((NSEM,)),
            pltpu.SemaphoreType.DMA((NSEM,)),
            pltpu.SemaphoreType.DMA((3,)),
            pltpu.SemaphoreType.DMA((5,)),
        ],
        compiler_params=pltpu.CompilerParams(
            collective_id=0, has_side_effects=True, vmem_limit_bytes=56 << 20
        ),
        name="swiglu",
    )(tokens.T, out_grad.T, gate_weight, up_weight, down_weight.T)
    outs = pl.pallas_call(
        hand_over,
        out_shape=tuple(jax.ShapeDtypeStruct(o.shape, o.dtype) for o in outs),
        in_specs=[hbm] * 5,
        out_specs=(hbm,) * 5,
        scratch_shapes=[V(o.shape, o.dtype) for o in outs] + [pltpu.SemaphoreType.DMA((2, 5))],
        name="hand_over",
    )(*outs)
    mixed, tgrad, gg, ug, dg = outs
    return mixed.T, tgrad.T, gg, ug, dg.T


def solution(mesh):
    placed = (P(None, "tp"), P("tp", "fsdp"), P("tp", "fsdp"), P("fsdp", "tp"), P(None, "tp"))
    return jax.shard_map(
        shards,
        mesh=mesh,
        in_specs=placed,
        out_specs=(P(None, "tp"), P(None, "tp"), P("tp", "fsdp"), P("tp", "fsdp"), P("fsdp", "tp")),
        check_vma=False,
    )
```

time: 125 us -> 99.8 us (0.80)
  Pallas kernels: 112 us -> 99 us
  local copies, waits for them, and re-layouts: 12.3 us -> 0 us
    pallas_call x1 -> x2, Pallas kernels: 112 us -> 99 us  [the longest x1 96.1 us: shards(): pl.pallas_call(kernel, out_shape=(jax.ShapeDtypeStruct((DM, TOKENS), BF),...]
    unnamed x13 -> x0, local copies, waits for them, and re-layouts: 7.28 us -> none
    pallas_call x3 -> x0, local copies, waits for them, and re-layouts: 5.06 us -> none  [shards(): pl.pallas_call(kernel, out_shape=(jax.ShapeDtypeStruct((TOKENS, DM), BF),...]
where the time goes in v2:
time: 99.8 us; the launch traced here: 99.6 us
  Pallas kernels  99 us (99%)
    pallas_call x1, Pallas kernels, shards(): pl.pallas_call(kernel, out_shape=(jax.ShapeDtypeStruct((DM, TOKENS), BF),...  96.1 us
    pallas_call x1, Pallas kernels, shards(): pl.pallas_call(hand_over, out_shape=tuple((jax.ShapeDtypeStruct(o.shape,...  2.93 us

profile of v2, /device:TPU:1, one launch (start us, length us, event | category | flops | bytes accessed | tf_op | source)
XLA Modules:
  0.0 99.6 jit_solution(11758636918905266955)
XLA Ops:
  0.6 96.1 %swiglu.1 = (bf16[288,512]{1,0:T(8,128)(2,1)}, bf16[288,512]{1,0:T(8,128)(2,1)}, f32[288,768]{1,0:T(8,128)}, f32[288,768]{1,0:T(8,128)}, f32[288,768]{1,0:T(8,128)}) custom-call(bf16[288,512]{1,0:T(8,128)(2,1)} %bitcast.7, bf16[288,512]{1,0:T(8,128)(2,1)} %bitcast.8, bf16[288,768]{1,0:T(8,128)(2,1)} %wg_h.1, bf16[288,768]{1,0:T(8,128)(2,1)} %wu_h.1, ...), custom_call_target="tpu_custom_call" | custom-call | tf_op jit(solution)/shard_map/swiglu/pallas_call | solution.py:364
  96.7 2.9 %hand_over.1 = (bf16[288,512]{1,0:T(8,128)(2,1)}, bf16[288,512]{1,0:T(8,128)(2,1)}, f32[288,768]{1,0:T(8,128)}, f32[288,768]{1,0:T(8,128)}, f32[288,768]{1,0:T(8,128)}) custom-call(bf16[288,512]{1,0:T(8,128)(2,1)} %get-tuple-element.15.refs_0_, bf16[288,512]{1,0:T(8,128)(2,1)} %get-tuple-element.16.refs_1_, f32[288,768]{1,0:T(8,128)} %get-tuple-element.17.refs_2_, ...), custom_call_target="tpu_custom_call" | custom-call | tf_op jit(solution)/shard_map/hand_over/pallas_call | solution.py:419

commit v3 on v2

--- a/solution.py
+++ b/solution.py
@@ -14,10 +14,13 @@
 NC = 2
 ROWS = TOKENS // NC
 U = ROWS // 16
-HALF = FF // 2
-W3 = 3 * HALF
+HID = (FF // 3, FF - FF // 3)
+AT = (0, HID[0])
+WIDE = tuple(3 * h for h in HID)
 Q = ROWS // 2
 NSEM = 45 * NC
+NOWN, OWN = 9, 32
+ZT = BF
 LAG, T_Y, T_X, T_CORE, T_XL, T_Z = 1.5, 4.0, 4.5, 2.5, 3.6, 5.0
 T_OPEN = (3.5, 5.0)
 
@@ -26,8 +29,8 @@
     return lax.dot_general(left, right, ((dims[:1], dims[1:]), ((), ())), preferred_element_type=F32)
 
 
-def gating(sums):
-    gate, up, back = sums[:, :HALF], sums[:, HALF : 2 * HALF], sums[:, 2 * HALF :]
+def gating(sums, n):
+    gate, up, back = sums[:, :n], sums[:, n : 2 * n], sums[:, 2 * n :]
     sig = jax.nn.sigmoid(gate)
     activated = gate * sig
     hidden = (activated * up).astype(BF)
@@ -39,9 +42,9 @@
 def kernel(
     tok_h, og_h, wg_h, wu_h, wd_h,
     mixed, tgrad, gg, ug, dg,
-    part, sb1, rb1, sf1, rf1, tx, xr, sx, rx, sb2, rb2, sf2, rf2, gat1, gat2,
-    wp, cr, av, xlr, bv, bs, zr, fin, gbuf, ubuf, dbuf, tok, og, tok_t, og_t, wg, wu, wd,
-    ss, rs, ls, ins,
+    part1, part2, sb1, rb1, sf1, rf1, tx, xr, sx, rx, sb2, rb2, sf2, rf2, gat1, gat2,
+    wp, cr, av, xlr, bv, zr, fin, zall, tok, og, tok_t, og_t, wg, wu, wd,
+    ss, rs, ins,
 ):
     tp, fs = lax.axis_index("tp"), lax.axis_index("fsdp")
     y, xh = tp // 2, tp % 2
@@ -85,27 +88,36 @@
             sent.append(copy)
         return copy
 
-    def group(whole):
-        i = count[0]
+    def alone():
         count[0] += 1
-        copy = pltpu.make_async_remote_copy(
+        return count[0] - 1
+
+    def tally(whole, i):
+        return pltpu.make_async_remote_copy(
             src_ref=whole, dst_ref=whole, send_sem=ss.at[i], recv_sem=rs.at[i], device_id=dev(dy=1), device_id_type=MESH
         )
+
+    def group(whole):
+        i = alone()
+        copy = tally(whole, i)
         sent.append(copy)
         return i, copy
 
     ZORDER = [6, 5, 7, 4, 8, 3, 9, 2, 10, 1, 11]
     KORDER = [4, 3, -3, 2, -2, 1, -1, 0]
 
+    parts = (part1, part2)
+
     def partial(st, c):
         rows = pl.ds(c * ROWS, ROWS)
-        cols = pl.ds(st * HALF, HALF)
+        n = HID[st]
+        cols = pl.ds(AT[st], n)
         for at, val in (
             (0, lambda: contract(tok[rows, :], wg[:, cols], (1, 0))),
             (1, lambda: contract(tok[rows, :], wu[:, cols], (1, 0))),
             (2, lambda: contract(og[rows, :], wd[:, cols], (1, 0))),
         ):
-            part[st, c, :, :, :, at * HALF : (at + 1) * HALF] = val().reshape(NY, 2, U, HALF)
+            parts[st][c, :, :, :, at * n : (at + 1) * n] = val().reshape(NY, 2, U, n)
 
     def chain(value, long, sb, rb, sf, rf):
         got = {}
@@ -143,9 +155,10 @@
                     continue
                 if s > 1:
                     got[sg].wait_recv()
-                    arrived(ymod(y - sg * (s - 1)))
                 at = slot(ymod(y - sg * (s - 1)))
                 got[sg] = send(at, at, dev(dy=sg))
+                if s > 1:
+                    arrived(ymod(y - sg * (s - 1)))
             yield T_Y
         got[long].wait_recv()
         arrived(ymod(y - long * 4))
@@ -153,16 +166,17 @@
         arrived(ymod(y + long * 3))
 
     def keep(at, sums):
-        hidden, gate_back, up_back = gating(sums)
-        at[:, :HALF] = hidden
-        at[:, HALF : 2 * HALF] = gate_back
-        at[:, 2 * HALF :] = up_back
+        n = sums.shape[1] // 3
+        hidden, gate_back, up_back = gating(sums, n)
+        at[:, :n] = hidden
+        at[:, n : 2 * n] = gate_back
+        at[:, 2 * n :] = up_back
 
     def stream0(c):
         long = 1 if c % 2 == 0 else -1
 
         def value(owner, _):
-            return part[0, c, owner]
+            return part1[c, owner]
 
         total = yield from chain(value, long, sb1.at[c], rb1.at[c], sf1.at[c], rf1.at[c])
         tx[c] = total
@@ -176,7 +190,7 @@
     def stream1_open(c, out, ks):
         for k in ks:
             off = KORDER[k]
-            sx[c, k] = part[1, c, ymod(y + off), 1 - xh].astype(BF)
+            sx[c, k] = part2[c, ymod(y + off), 1 - xh].astype(BF)
             out[off] = send(sx.at[c, k], rx.at[c, k], dev(dxh=1))
 
     def stream1(c, from_x):
@@ -189,7 +203,7 @@
                 from_x[off].wait_recv()
                 ready.add(off)
             k = KORDER.index(off)
-            return part[1, c, owner, xh] + rx[c, k].astype(F32)
+            return part2[c, owner, xh] + rx[c, k].astype(F32)
 
         yield T_OPEN[c]
         total = yield from chain(value, long, sb2.at[c], rb2.at[c], sf2.at[c], rf2.at[c])
@@ -207,19 +221,15 @@
     grads = []
 
     def weight_grad(i):
-        left, cols, out, to = (
-            (tok_t, 1, gbuf, gg),
-            (tok_t, 2, ubuf, ug),
-            (og_t, 0, dbuf, dg),
+        left, cols, out = (
+            (tok_t, 1, gg),
+            (tok_t, 2, ug),
+            (og_t, 0, dg),
         )[i]
         for st, g in ((0, gat1), (1, gat2)):
-            right = g[:, :, :, :, cols * HALF : (cols + 1) * HALF].reshape(TOKENS, HALF)
-            out[:, st * HALF : (st + 1) * HALF] = contract(left[...], right, (1, 0))
-        copy = pltpu.make_async_copy(out, to, ls.at[i])
-        copy.start()
-        local.append(copy)
-
-    local = []
+            n = HID[st]
+            right = g[:, :, :, :, cols * n : (cols + 1) * n].reshape(TOKENS, n)
+            out[:, AT[st] : AT[st] + n] = contract(left[...], right, (1, 0))
 
     def weight_grads():
         for i in range(3):
@@ -235,8 +245,9 @@
         def side(weights, at):
             total = None
             for st, g in ((0, gat1), (1, gat2)):
-                left = weights[:, st * HALF : (st + 1) * HALF]
-                right = g[c, :, :, :, at * HALF : (at + 1) * HALF].reshape(ROWS, HALF)
+                n = HID[st]
+                left = weights[:, AT[st] : AT[st] + n]
+                right = g[c, :, :, :, at * n : (at + 1) * n].reshape(ROWS, n)
                 one = contract(left, right, (1, 1))
                 total = one if total is None else total + one
             return total
@@ -256,26 +267,45 @@
         wp[c, co, xl] = own
         yield T_XL
         got.wait_recv()
-        own = (wp[c, co, xl] + xlr[c].astype(F32)).reshape(NZ, DM // NZ, Q)
-        bv[c] = own
-        bs[c, :, : DM // NZ] = own.astype(BF)
-        i, got = group(zr.at[c])
+        own = (wp[c, co, xl] + xlr[c].astype(F32)).reshape(NOWN, OWN, Q)
+        bv[c] = own.astype(ZT)
+        i = alone()
         for d in ZORDER:
-            send(bs.at[c, lax.rem(z + d, NZ)], zr.at[c, d - 1], dev(dz=d), i)
+            zt = lax.rem(z + d, NZ)
+
+            @pl.when(zt % 4 != 3)
+            def _(d=d, zt=zt):
+                send(bv.at[c, zt - zt // 4], zr.at[c, d - 1], dev(dz=d), i)
+
+        k = alone()
+        mine = fin.at[c, co, xl, z - z // 4]
         flush(c)
         yield T_Z
-        total = bv[c, z]
-        got.wait_recv()
-        for d in range(1, NZ):
-            total = total + zr[c, d - 1, : DM // NZ].astype(F32)
-        fin[c, co, xl, z, : DM // NZ] = total.astype(BF)
-        mine = fin.at[c, co, xl, z]
-        i, got = group(fin.at[c, co, xl, : NZ - 1])
-        for d in ZORDER:
-            send(mine, mine, dev(dz=d), i)
+
+        @pl.when(z % 4 != 3)
+        def _():
+            tally(zr.at[c], i).wait_recv()
+            total = bv[c, z - z // 4].astype(F32)
+            for d in range(1, NZ):
+                total = total + zr[c, d - 1].astype(F32)
+            fin[c, co, xl, z - z // 4] = total.astype(BF)
+            for d in ZORDER:
+                send(mine, mine, dev(dz=d), k)
+
         flush(c)
         yield T_Z
-        got.wait_recv()
+
+        @pl.when(z % 4 != 3)
+        def _():
+            tally(fin.at[c, co, xl, : NOWN - 1], k).wait_recv()
+            tally(bv.at[c, : NOWN - 1], i).wait_send()
+            tally(zall.at[c], k).wait_send()
+
+        @pl.when(z % 4 == 3)
+        def _():
+            tally(fin.at[c, co, xl], k).wait_recv()
+            tally(bv.at[c], i).wait_send()
+
         mine = fin.at[c, co, xl]
         across = send(mine, mine, dev(dxl=1))
         near = send(mine, mine, dev(dco=1))
@@ -289,7 +319,7 @@
         far.wait_recv()
         for m, out in ((0, mixed), (1, tgrad)):
             for h in range(2):
-                block = fin[c, m, h, :, : DM // NZ].reshape(DM, Q)
+                block = fin[c, m, h].reshape(DM, Q)
                 out[:, c * ROWS + h * Q : c * ROWS + (h + 1) * Q] = block
 
     queue = []
@@ -322,8 +352,6 @@
         if c == NC - 1:
             for other in range(NC):
                 stream1_open(other, opened[other], range(5, NY))
-            fin[...] = jnp.zeros_like(fin)
-            bs[...] = jnp.zeros_like(bs)
 
     for c in range(NC):
         push(c * LAG, opening(c, c * LAG), c, False)
@@ -340,20 +368,13 @@
                         push(t + 0.1, weight_grads(), NC, False)
     for copy in sent:
         copy.wait_send()
-    for copy in local:
-        copy.wait()
 
 
 def hand_over(*refs):
-    held, sems = refs[10:15], refs[15]
-    into = [pltpu.make_async_copy(refs[i], held[i], sems.at[0, i]) for i in range(5)]
-    out = [pltpu.make_async_copy(held[i], refs[5 + i], sems.at[1, i]) for i in range(5)]
-    for copy in into:
+    copies = [pltpu.make_async_copy(refs[i], refs[5 + i], refs[10].at[i]) for i in range(5)]
+    for copy in copies:
         copy.start()
-    for first, second in zip(into, out):
-        first.wait()
-        second.start()
-    for copy in out:
+    for copy in copies:
         copy.wait()
 
 
@@ -364,41 +385,39 @@
     outs = pl.pallas_call(
         kernel,
         out_shape=(
-            jax.ShapeDtypeStruct((DM, TOKENS), BF),
-            jax.ShapeDtypeStruct((DM, TOKENS), BF),
-            jax.ShapeDtypeStruct((DM, FF), F32),
-            jax.ShapeDtypeStruct((DM, FF), F32),
-            jax.ShapeDtypeStruct((DM, FF), F32),
+            V((DM, TOKENS), BF),
+            V((DM, TOKENS), BF),
+            V((DM, FF), F32),
+            V((DM, FF), F32),
+            V((DM, FF), F32),
         ),
         in_specs=[hbm] * 5,
-        out_specs=(vm, vm, hbm, hbm, hbm),
+        out_specs=(vm,) * 5,
         scratch_shapes=[
-            V((2, NC, NY, 2, U, W3), F32),
-            V((NC, 2, 3, 2, U, W3), BF),
-            V((NC, 2, 3, 2, U, W3), BF),
-            V((NC, 2, 2, U, W3), F32),
-            V((NC, 2, 2, U, W3), F32),
-            V((NC, 2, U, W3), F32),
-            V((NC, 2, U, W3), F32),
-            V((NC, NY, U, W3), BF),
-            V((NC, NY, U, W3), BF),
-            V((NC, 2, 3, U, W3), BF),
-            V((NC, 2, 3, U, W3), BF),
-            V((NC, 2, U, W3), F32),
-            V((NC, 2, U, W3), F32),
-            V((NC, NY, 2, U, W3), BF),
-            V((NC, NY, 2, U, W3), BF),
+            V((NC, NY, 2, U, WIDE[0]), F32),
+            V((NC, NY, 2, U, WIDE[1]), F32),
+            V((NC, 2, 3, 2, U, WIDE[0]), BF),
+            V((NC, 2, 3, 2, U, WIDE[0]), BF),
+            V((NC, 2, 2, U, WIDE[0]), F32),
+            V((NC, 2, 2, U, WIDE[0]), F32),
+            V((NC, 2, U, WIDE[0]), F32),
+            V((NC, 2, U, WIDE[0]), F32),
+            V((NC, NY, U, WIDE[1]), BF),
+            V((NC, NY, U, WIDE[1]), BF),
+            V((NC, 2, 3, U, WIDE[1]), BF),
+            V((NC, 2, 3, U, WIDE[1]), BF),
+            V((NC, 2, U, WIDE[1]), F32),
+            V((NC, 2, U, WIDE[1]), F32),
+            V((NC, NY, 2, U, WIDE[0]), BF),
+            V((NC, NY, 2, U, WIDE[1]), BF),
             V((NC, 2, 2, DM, Q), F32),
             V((NC, 2, DM, Q), F32),
             V((NC, DM, Q), BF),
             V((NC, DM, Q), BF),
-            V((NC, NZ, DM // NZ, Q), F32),
-            V((NC, NZ, 32, Q), BF),
-            V((NC, NZ - 1, 32, Q), BF),
-            V((NC, 2, 2, NZ, 32, Q), BF),
-            V((DM, FF), F32),
-            V((DM, FF), F32),
-            V((DM, FF), F32),
+            V((NC, NOWN, OWN, Q), ZT),
+            V((NC, NZ - 1, OWN, Q), ZT),
+            V((NC, 2, 2, NOWN, OWN, Q), BF),
+            V((NC, NZ - 1, OWN, Q), BF),
             V((TOKENS, DM), BF),
             V((TOKENS, DM), BF),
             V((DM, TOKENS), BF),
@@ -408,7 +427,6 @@
             V((DM, FF), BF),
             pltpu.SemaphoreType.DMA((NSEM,)),
             pltpu.SemaphoreType.DMA((NSEM,)),
-            pltpu.SemaphoreType.DMA((3,)),
             pltpu.SemaphoreType.DMA((5,)),
         ],
         compiler_params=pltpu.CompilerParams(
@@ -416,12 +434,13 @@
         ),
         name="swiglu",
     )(tokens.T, out_grad.T, gate_weight, up_weight, down_weight.T)
+    outs = [pltpu.with_memory_space_constraint(o, pltpu.VMEM) for o in outs]
     outs = pl.pallas_call(
         hand_over,
         out_shape=tuple(jax.ShapeDtypeStruct(o.shape, o.dtype) for o in outs),
         in_specs=[hbm] * 5,
         out_specs=(hbm,) * 5,
-        scratch_shapes=[V(o.shape, o.dtype) for o in outs] + [pltpu.SemaphoreType.DMA((2, 5))],
+        scratch_shapes=[pltpu.SemaphoreType.DMA((5,))],
         name="hand_over",
     )(*outs)
     mixed, tgrad, gg, ug, dg = outs

time: 99.8 us -> 95 us (0.952)
  Pallas kernels: 99 us -> 94.2 us
    pallas_call x1, Pallas kernels: 96.1 us -> 92.5 us  [shards(): pl.pallas_call(kernel, out_shape=(V((DM, TOKENS), BF), V((DM, TOKENS), BF...]
    pallas_call x1, Pallas kernels: 2.93 us -> 1.73 us  [shards(): pl.pallas_call(hand_over, out_shape=tuple((jax.ShapeDtypeStruct(o.shape,...]
where the time goes in v3:
time: 95 us; the launch traced here: 94.9 us
  Pallas kernels  94.2 us (99%)
    pallas_call x1, Pallas kernels, shards(): pl.pallas_call(kernel, out_shape=(V((DM, TOKENS), BF), V((DM, TOKENS), BF...  92.5 us

profile of v3, /device:TPU:1, one launch (start us, length us, event | category | flops | bytes accessed | tf_op | source)
XLA Modules:
  0.0 94.9 jit_solution(15470851015925509402)
XLA Ops:
  0.6 92.5 %swiglu.1 = (bf16[288,512]{1,0:T(8,128)(2,1)S(1)}, bf16[288,512]{1,0:T(8,128)(2,1)S(1)}, f32[288,768]{1,0:T(8,128)S(1)}, f32[288,768]{1,0:T(8,128)S(1)}, f32[288,768]{1,0:T(8,128)S(1)}) custom-call(bf16[288,512]{1,0:T(8,128)(2,1)} %bitcast.7, bf16[288,512]{1,0:T(8,128)(2,1)} %bitcast.8, bf16[288,768]{1,0:T(8,128)(2,1)} %wg_h.1, bf16[288,768]{1,0:T(8,128)(2,1)} %wu_h.1, ...), custom_call_target="tpu_custom_call" | custom-call | tf_op jit(solution)/shard_map/swiglu/pallas_call | solution.py:385
  93.1 1.7 %hand_over.1 = (bf16[288,512]{1,0:T(8,128)(2,1)}, bf16[288,512]{1,0:T(8,128)(2,1)}, f32[288,768]{1,0:T(8,128)}, f32[288,768]{1,0:T(8,128)}, f32[288,768]{1,0:T(8,128)}) custom-call(bf16[288,512]{1,0:T(8,128)(2,1)S(1)} %get-tuple-element.15.refs_0_, bf16[288,512]{1,0:T(8,128)(2,1)S(1)} %get-tuple-element.16.refs_1_, ...), custom_call_target="tpu_custom_call" | custom-call | tf_op jit(solution)/shard_map/hand_over/pallas_call | solution.py:438

commit v4 on v3

--- a/solution.py
+++ b/solution.py
@@ -18,9 +18,8 @@
 AT = (0, HID[0])
 WIDE = tuple(3 * h for h in HID)
 Q = ROWS // 2
-NSEM = 45 * NC
+NSEND, NRECV = 16 * NC, 45 * NC
 NOWN, OWN = 9, 32
-ZT = BF
 LAG, T_Y, T_X, T_CORE, T_XL, T_Z = 1.5, 4.0, 4.5, 2.5, 3.6, 5.0
 T_OPEN = (3.5, 5.0)
 
@@ -43,7 +42,7 @@
     tok_h, og_h, wg_h, wu_h, wd_h,
     mixed, tgrad, gg, ug, dg,
     part1, part2, sb1, rb1, sf1, rf1, tx, xr, sx, rx, sb2, rb2, sf2, rf2, gat1, gat2,
-    wp, cr, av, xlr, bv, zr, fin, zall, tok, og, tok_t, og_t, wg, wu, wd,
+    wp, cr, av, xlr, bv, bw, zr, fin, zall, tok, og, tok_t, og_t, wg, wu, wd,
     ss, rs, ins,
 ):
     tp, fs = lax.axis_index("tp"), lax.axis_index("fsdp")
@@ -75,33 +74,38 @@
         loads[name].start()
 
     sent = []
-    count = [0]
-
-    def send(src, dst, to, at=None):
-        i = count[0] if at is None else at
-        count[0] += at is None
+    used = [0, 0]
+
+    def fresh(side):
+        used[side] += 1
+        return used[side] - 1
+
+    def send(src, dst, to, at=None, out=None):
+        if at is not None:
+            o, i = at
+        else:
+            o, i = fresh(0) if out is None else out, fresh(1)
         copy = pltpu.make_async_remote_copy(
-            src_ref=src, dst_ref=dst, send_sem=ss.at[i], recv_sem=rs.at[i], device_id=to, device_id_type=MESH
+            src_ref=src, dst_ref=dst, send_sem=ss.at[o], recv_sem=rs.at[i], device_id=to, device_id_type=MESH
         )
         copy.start()
-        if at is None:
+        if at is None and out is None:
             sent.append(copy)
         return copy
 
     def alone():
-        count[0] += 1
-        return count[0] - 1
-
-    def tally(whole, i):
+        return fresh(0), fresh(1)
+
+    def tally(whole, at):
         return pltpu.make_async_remote_copy(
-            src_ref=whole, dst_ref=whole, send_sem=ss.at[i], recv_sem=rs.at[i], device_id=dev(dy=1), device_id_type=MESH
+            src_ref=whole, dst_ref=whole, send_sem=ss.at[at[0]], recv_sem=rs.at[at[1]], device_id=dev(dy=1), device_id_type=MESH
         )
 
     def group(whole):
-        i = alone()
-        copy = tally(whole, i)
+        at = alone()
+        copy = tally(whole, at)
         sent.append(copy)
-        return i, copy
+        return at, copy
 
     ZORDER = [6, 5, 7, 4, 8, 3, 9, 2, 10, 1, 11]
     KORDER = [4, 3, -3, 2, -2, 1, -1, 0]
@@ -119,8 +123,9 @@
         ):
             parts[st][c, :, :, :, at * n : (at + 1) * n] = val().reshape(NY, 2, U, n)
 
-    def chain(value, long, sb, rb, sf, rf):
+    def chain(value, long, sb, rb, sf, rf, five):
         got = {}
+        narrow, wide = fresh(0), fresh(0)
         todo = {}
         for sg, d in ((1, 0), (-1, 1)):
             first = 1 if sg == long else 2
@@ -138,17 +143,19 @@
                     val = val + rb[d, s - 2].astype(F32)
                 if s == 4:
                     sf[d] = val
-                    got[sg] = send(sf.at[d], rf.at[d], dev(dy=sg))
+                    got[sg] = send(sf.at[d], rf.at[d], dev(dy=sg), out=wide)
                 else:
                     sb[d, s - 1] = val.astype(BF)
-                    got[sg] = send(sb.at[d, s - 1], rb.at[d, s - 1], dev(dy=sg))
+                    got[sg] = send(sb.at[d, s - 1], rb.at[d, s - 1], dev(dy=sg), out=narrow)
             yield T_Y
         for sg in (1, -1):
             got[sg].wait_recv()
+        sent.extend((tally(five, (narrow, 0)), tally(sf, (wide, 0))))
         return value(y, 0) + rf[0] + rf[1]
 
-    def spread(slot, long, arrived):
+    def spread(slot, long, arrived, seven):
         got = {}
+        out = fresh(0)
         for s in range(1, 5):
             for sg in (1, -1):
                 if s == 4 and sg != long:
@@ -156,7 +163,7 @@
                 if s > 1:
                     got[sg].wait_recv()
                 at = slot(ymod(y - sg * (s - 1)))
-                got[sg] = send(at, at, dev(dy=sg))
+                got[sg] = send(at, at, dev(dy=sg), out=out)
                 if s > 1:
                     arrived(ymod(y - sg * (s - 1)))
             yield T_Y
@@ -164,6 +171,7 @@
         arrived(ymod(y - long * 4))
         got[-long].wait_recv()
         arrived(ymod(y + long * 3))
+        sent.append(tally(seven, (out, 0)))
 
     def keep(at, sums):
         n = sums.shape[1] // 3
@@ -178,20 +186,26 @@
         def value(owner, _):
             return part1[c, owner]
 
-        total = yield from chain(value, long, sb1.at[c], rb1.at[c], sf1.at[c], rf1.at[c])
+        total = yield from chain(value, long, sb1.at[c], rb1.at[c], sf1.at[c], rf1.at[c], gat1.at[c, :5])
         tx[c] = total
         got = send(tx.at[c], xr.at[c], dev(dxh=1))
         yield T_X
         got.wait_recv()
         for h in range(2):
             keep(gat1.at[c, y, h], tx[c, h] + xr[c, h])
-        yield from spread(lambda o: gat1.at[c, o], long, lambda o: None)
+        yield from spread(lambda o: gat1.at[c, o], long, lambda o: None, gat1.at[c, :7])
+
+    xsem = {}
 
     def stream1_open(c, out, ks):
         for k in ks:
             off = KORDER[k]
             sx[c, k] = part2[c, ymod(y + off), 1 - xh].astype(BF)
-            out[off] = send(sx.at[c, k], rx.at[c, k], dev(dxh=1))
+            if not out:
+                xsem[c] = fresh(0)
+            out[off] = send(sx.at[c, k], rx.at[c, k], dev(dxh=1), out=xsem[c])
+            if k == NY - 1:
+                sent.append(tally(sx.at[c], (xsem[c], 0)))
 
     def stream1(c, from_x):
         long = -1 if c % 2 == 0 else 1
@@ -206,7 +220,7 @@
             return part2[c, owner, xh] + rx[c, k].astype(F32)
 
         yield T_OPEN[c]
-        total = yield from chain(value, long, sb2.at[c], rb2.at[c], sf2.at[c], rf2.at[c])
+        total = yield from chain(value, long, sb2.at[c], rb2.at[c], sf2.at[c], rf2.at[c], sx.at[c, :5])
         keep(gat2.at[c, y, xh], total)
         i, back = group(gat2.at[c, :, 1 - xh])
 
@@ -214,7 +228,7 @@
             send(gat2.at[c, o, xh], gat2.at[c, o, xh], dev(dxh=1), i)
 
         arrived(y)
-        yield from spread(lambda o: gat2.at[c, o, xh], long, arrived)
+        yield from spread(lambda o: gat2.at[c, o, xh], long, arrived, sx.at[c, :7])
         yield T_X
         back.wait_recv()
 
@@ -238,7 +252,7 @@
 
     def flush(c):
         if c == NC - 1:
-            while len(sent) > 20:
+            while len(sent) > 8:
                 sent.pop(0).wait_send()
 
     def reduce(c):
@@ -261,14 +275,15 @@
         got = send(wp.at[c, 1 - co], cr.at[c], dev(dco=1))
         yield T_CORE
         got.wait_recv()
-        av[c] = (wp[c, co, 1 - xl] + cr[c, 1 - xl]).astype(BF)
+        av[c] = wp[c, co, 1 - xl] + cr[c, 1 - xl]
         got = send(av.at[c], xlr.at[c], dev(dxl=1))
         own = wp[c, co, xl] + cr[c, xl]
         wp[c, co, xl] = own
         yield T_XL
         got.wait_recv()
-        own = (wp[c, co, xl] + xlr[c].astype(F32)).reshape(NOWN, OWN, Q)
-        bv[c] = own.astype(ZT)
+        own = (wp[c, co, xl] + xlr[c]).reshape(NOWN, OWN, Q)
+        bv[c] = own.astype(BF)
+        bw[c] = own
         i = alone()
         for d in ZORDER:
             zt = lax.rem(z + d, NZ)
@@ -285,7 +300,7 @@
         @pl.when(z % 4 != 3)
         def _():
             tally(zr.at[c], i).wait_recv()
-            total = bv[c, z - z // 4].astype(F32)
+            total = bw[c, z - z // 4]
             for d in range(1, NZ):
                 total = total + zr[c, d - 1].astype(F32)
             fin[c, co, xl, z - z // 4] = total.astype(BF)
@@ -412,10 +427,11 @@
             V((NC, NY, 2, U, WIDE[1]), BF),
             V((NC, 2, 2, DM, Q), F32),
             V((NC, 2, DM, Q), F32),
-            V((NC, DM, Q), BF),
-            V((NC, DM, Q), BF),
-            V((NC, NOWN, OWN, Q), ZT),
-            V((NC, NZ - 1, OWN, Q), ZT),
+            V((NC, DM, Q), F32),
+            V((NC, DM, Q), F32),
+            V((NC, NOWN, OWN, Q), BF),
+            V((NC, NOWN, OWN, Q), F32),
+            V((NC, NZ - 1, OWN, Q), BF),
             V((NC, 2, 2, NOWN, OWN, Q), BF),
             V((NC, NZ - 1, OWN, Q), BF),
             V((TOKENS, DM), BF),
@@ -425,8 +441,8 @@
             V((DM, FF), BF),
             V((DM, FF), BF),
             V((DM, FF), BF),
-            pltpu.SemaphoreType.DMA((NSEM,)),
-            pltpu.SemaphoreType.DMA((NSEM,)),
+            pltpu.SemaphoreType.DMA((NSEND,)),
+            pltpu.SemaphoreType.DMA((NRECV,)),
             pltpu.SemaphoreType.DMA((5,)),
         ],
         compiler_params=pltpu.CompilerParams(

time: 95 us -> 96.2 us (1.013)
  Pallas kernels: 94.2 us -> 95.4 us
    pallas_call x1, Pallas kernels: 92.5 us -> 93.7 us  [shards(): pl.pallas_call(kernel, out_shape=(V((DM, TOKENS), BF), V((DM, TOKENS), BF...]
where the time goes in v4:
time: 96.2 us; the launch traced here: 96.1 us
  Pallas kernels  95.4 us (99%)
    pallas_call x1, Pallas kernels, shards(): pl.pallas_call(kernel, out_shape=(V((DM, TOKENS), BF), V((DM, TOKENS), BF...  93.7 us

profile of v4, /device:TPU:1, one launch (start us, length us, event | category | flops | bytes accessed | tf_op | source)
XLA Modules:
  0.0 96.1 jit_solution(12004886280881553505)
XLA Ops:
  0.6 93.7 %swiglu.1 = (bf16[288,512]{1,0:T(8,128)(2,1)S(1)}, bf16[288,512]{1,0:T(8,128)(2,1)S(1)}, f32[288,768]{1,0:T(8,128)S(1)}, f32[288,768]{1,0:T(8,128)S(1)}, f32[288,768]{1,0:T(8,128)S(1)}) custom-call(bf16[288,512]{1,0:T(8,128)(2,1)} %bitcast.7, bf16[288,512]{1,0:T(8,128)(2,1)} %bitcast.8, bf16[288,768]{1,0:T(8,128)(2,1)} %wg_h.1, bf16[288,768]{1,0:T(8,128)(2,1)} %wu_h.1, ...), custom_call_target="tpu_custom_call" | custom-call | tf_op jit(solution)/shard_map/swiglu/pallas_call | solution.py:400
  94.4 1.7 %hand_over.1 = (bf16[288,512]{1,0:T(8,128)(2,1)}, bf16[288,512]{1,0:T(8,128)(2,1)}, f32[288,768]{1,0:T(8,128)}, f32[288,768]{1,0:T(8,128)}, f32[288,768]{1,0:T(8,128)}) custom-call(bf16[288,512]{1,0:T(8,128)(2,1)S(1)} %get-tuple-element.15.refs_0_, bf16[288,512]{1,0:T(8,128)(2,1)S(1)} %get-tuple-element.16.refs_1_, ...), custom_call_target="tpu_custom_call" | custom-call | tf_op jit(solution)/shard_map/hand_over/pallas_call | solution.py:454
